TPU v7x, 256 devices: a whole 4x4x8 slice. The times are simulated.
256 devices in a mesh: batch: 8 (over y, core), gx: 8 (over z), gy: 4 (over x).
Axes of the slice: x: 4, y: 4, z: 8, core: 2. Of those that a mesh axis runs over, the one named last changes fastest.
Arguments:
- tokens: bfloat16 [512, 2, 18432], P(None, None, ('batch', 'gy')), may hold values from -6 to 6
- w_query: bfloat16 [18432, 12288], P(('batch', 'gy'), 'gx'), may hold values from -0.046875 to 0.046875
- w_keyval: bfloat16 [18432, 512], P(('batch', 'gy'), 'gx'), may hold values from -0.09375 to 0.09375
- w_out: bfloat16 [12288, 18432], P('gx', ('batch', 'gy')), may hold values from -0.19921875 to 0.19921875
- cache_keys: bfloat16 [512, 2048, 256], P(('batch', 'gx', 'gy')), may hold values from -140 to 140
- cache_values: bfloat16 [512, 2048, 256], P(('batch', 'gx', 'gy')), may hold values from -6 to 6
- lengths: int32 [512], P(('batch', 'gx', 'gy')), may hold values from 512 to 2048, as said below
Outputs:
- mixed: bfloat16 [512, 2, 18432], P('gx', None, ('batch', 'gy'))
Inputs may be any that keep to these rules, and one draw needn't show every extreme that they name: `lengths`: every draw has a sequence with 2048 valid positions and one with 512.
All inputs are finite; a program needn't handle non-finite values.
Results may differ from a plain program's by a relative error of at most 0.02.
Values may be sent and summed in bfloat16 or wider, within the bound.
A program may use at most 64 MiB of HBM per device.

v0:
```python
import jax
import jax.numpy as jnp
from jax import lax
from jax.sharding import PartitionSpec as P


def rotate(values, positions):
    half_width = values.shape[-1] // 2
    freqs = 10000.0 ** (-(jnp.arange(half_width, dtype=jnp.float32) * 2.0 / values.shape[-1]))
    angles = positions[..., None] * freqs
    cosine = jnp.cos(angles)
    sine = jnp.sin(angles)
    first_half = values[..., :half_width]
    second_half = values[..., half_width:]
    return jnp.concatenate(
        [first_half * cosine - second_half * sine, second_half * cosine + first_half * sine],
        axis=-1,
    )


def attend(queries, keys_cache, values_cache, new_keys, new_values, length_now):
    scaling = 1.0 / queries.shape[-1] ** 0.5
    cached = (
        jnp.einsum("thd,sd->ths", queries, keys_cache, preferred_element_type=jnp.float32) * scaling
    )
    valid = jnp.arange(keys_cache.shape[0], dtype=jnp.int32) < length_now
    cached = jnp.where(valid[None, None, :], cached, -1e30)
    fresh = (
        jnp.einsum("thd,ud->thu", queries, new_keys, preferred_element_type=jnp.float32) * scaling
    )
    steps_here = queries.shape[0]
    causal = jnp.arange(steps_here)[None, :] <= jnp.arange(steps_here)[:, None]
    fresh = jnp.where(causal[:, None, :], fresh, -1e30)
    highest = jnp.maximum(cached.max(-1, keepdims=True), fresh.max(-1, keepdims=True))
    exp_cached = jnp.exp(cached - highest)
    exp_fresh = jnp.exp(fresh - highest)
    denom = exp_cached.sum(-1, keepdims=True) + exp_fresh.sum(-1, keepdims=True)
    probs_cached = (exp_cached / denom).astype(jnp.bfloat16)
    probs_fresh = (exp_fresh / denom).astype(jnp.bfloat16)
    result = jnp.einsum(
        "ths,sd->thd", probs_cached, values_cache, preferred_element_type=jnp.float32
    )
    result = result + jnp.einsum(
        "thu,ud->thd", probs_fresh, new_values, preferred_element_type=jnp.float32
    )
    return result.reshape(steps_here, -1).astype(jnp.bfloat16)


def local(tokens, w_query, w_keyval, w_out, cache_keys, cache_values, lengths):
    batch_count = lax.axis_size("batch")
    first_count = lax.axis_size("gx")
    second_count = lax.axis_size("gy")
    owned_seqs = cache_keys.shape[0]
    head_width = cache_keys.shape[2]
    sequences, decode_steps, local_width = tokens.shape
    query_cols = w_query.shape[1]
    pair_cols = w_keyval.shape[1]
    head_total = query_cols * first_count // head_width
    arranged = tokens.reshape(
        batch_count, first_count, second_count * owned_seqs, decode_steps, local_width
    )
    arranged = arranged.transpose(0, 2, 1, 3, 4).reshape(
        batch_count * second_count * owned_seqs, first_count, decode_steps, local_width
    )
    joined = jnp.concatenate([w_query, w_keyval], axis=1)
    summed = lax.psum_scatter(
        jnp.einsum("rgtd,dc->rgtc", arranged, joined, preferred_element_type=jnp.float32),
        ("batch", "gy"),
        scatter_dimension=0,
        tiled=True,
    ).astype(jnp.bfloat16)
    owned = lax.all_to_all(summed, "gx", split_axis=1, concat_axis=3, tiled=True)
    owned = owned.reshape(owned_seqs, decode_steps, first_count, query_cols + pair_cols)
    queries = owned[..., :query_cols].reshape(owned_seqs, decode_steps, head_total, head_width)
    key_value = owned[..., query_cols:].reshape(owned_seqs, decode_steps, first_count * pair_cols)
    new_keys = key_value[..., :head_width]
    new_values = key_value[..., head_width:]
    positions = (lengths[:, None] + jnp.arange(decode_steps, dtype=jnp.int32)[None, :]).astype(
        jnp.float32
    )
    rot_queries = rotate(queries.astype(jnp.float32), positions[:, :, None]).astype(jnp.bfloat16)
    rot_keys = rotate(new_keys.astype(jnp.float32), positions).astype(jnp.bfloat16)
    attended = jax.vmap(attend)(
        rot_queries, cache_keys, cache_values, rot_keys, new_values, lengths
    )
    everyone = lax.all_gather(attended, ("batch", "gy"), axis=0, tiled=True)
    grouped = lax.all_to_all(everyone[None], "gx", split_axis=3, concat_axis=0, tiled=True)
    terms = jnp.einsum("grtc,cd->grtd", grouped, w_out, preferred_element_type=jnp.float32)
    ordered = terms.reshape(
        first_count, batch_count, second_count * owned_seqs, decode_steps, local_width
    )
    ordered = ordered.transpose(1, 0, 2, 3, 4).reshape(sequences, decode_steps, local_width)
    return lax.psum_scatter(ordered.astype(jnp.bfloat16), "gx", scatter_dimension=0, tiled=True)


def solution(mesh):
    placed = (
        P(None, None, ("batch", "gy")),
        P(("batch", "gy"), "gx"),
        P(("batch", "gy"), "gx"),
        P("gx", ("batch", "gy")),
        P(("batch", "gx", "gy"), None, None),
        P(("batch", "gx", "gy"), None, None),
        P(("batch", "gx", "gy")),
    )
    return jax.shard_map(
        local, mesh=mesh, in_specs=placed, out_specs=P("gx", None, ("batch", "gy")), check_vma=False
    )
```

profile of v0, /device:TPU:32, one launch (start us, length us, event | category | flops | bytes accessed | tf_op | source)
XLA Modules:
  0.0 359.1 jit_solution(5368077134398461354)
XLA Ops:
  6.5 1.8 copy.54
  8.4 1.2 copy.55
  9.6 0.1 copy.53
  9.8 5.0 %convolution_bitcast_fusion = f32[64,8,2,1600]{3,0,2,1:T(8,128)S(1)} fusion(bf16[576,64]{1,0:T(8,128)(2,1)S(1)} %copy.53, bf16[576,1536]{1,0:T(8,128)(2,1)} %param.8, bf16[64,8,2,576]{3,1,2,0:T(8,128)(2,1)} %bitcast.77), kind=kOutput, calls=%fused_computation | convolution fusion | flops 1891123200 | bytes 9576448 | tf_op jit(solution)/shard_map/rgtd,dc->rgtc/dot_general | solution.py:67
  14.8 6.7 %copy.57 = f32[64,8,2,1600]{3,1,2,0:T(8,128)} copy(f32[64,8,2,1600]{3,0,2,1:T(8,128)S(1)} %convolution_bitcast_fusion) | data formatting | bytes 13107200 | tf_op jit(solution)/shard_map/rgtd,dc->rgtc/dot_general | solution.py:67
  21.6 0.6 copy-done.2
  22.2 0.1 iota_compare_fusion
  22.2 96.8 %reduce-scatter.3.cloned.1.call-done = f32[2,8,2,1600]{3,1,2,0:T(8,128)} async-done(((f32[64,8,2,1600]{3,1,2,0:T(8,128)}), f32[2,8,2,1600]{3,1,2,0:T(8,128)}) %reduce-scatter.3.cloned.1.call-update) | async-done | bytes 204816 | tf_op jit(solution)/shard_map/reduce_scatter | solution.py:66
  119.1 0.9 convert_element_type.46
  120.0 0.7 copy.58
  120.7 7.5 %all-to-all-start = ((bf16[2,8,2,1600]{3,2,0,1:T(2,128)(2,1)}), bf16[2,8,2,1600]{3,2,0,1:T(2,128)(2,1)S(1)}, u32[]{:S(2)}, u32[]{:S(2)}) async-start(bf16[2,8,2,1600]{3,2,0,1:T(2,128)(2,1)} %copy.58), calls=%async_computation.1 | async-start | bytes 212992 | tf_op jit(solution)/shard_map/all_to_all | solution.py:72
  128.2 0.1 add_convert_fusion.2
  128.3 7.3 %all-to-all-done = bf16[2,8,2,1600]{3,2,0,1:T(2,128)(2,1)S(1)} async-done(((bf16[2,8,2,1600]{3,2,0,1:T(2,128)(2,1)}), bf16[2,8,2,1600]{3,2,0,1:T(2,128)(2,1)S(1)}, u32[]{:S(2)}, u32[]{:S(2)}) %all-to-all-start) | async-done | bytes 102432 | tf_op jit(solution)/shard_map/all_to_all | solution.py:72
  135.6 0.1 reshape.117
  135.8 0.1 subtract_convert_fusion.1
  136.0 0.9 fusion.39
  136.8 0.2 fusion.40
  137.0 0.4 fusion.19
  137.4 0.2 fusion.31
  137.6 0.6 fusion.24
  138.2 0.7 convert_element_type.54
  138.9 0.0 reduce-scatter.5.cloned.1.call-start
  138.9 45.4 %all-gather.2.cloned.1.call-done = bf16[64,2,12288]{2,1,0:T(2,128)(2,1)} async-done(((bf16[2,2,12288]{2,1,0:T(2,128)(2,1)}), bf16[64,2,12288]{2,1,0:T(2,128)(2,1)}) %all-gather.2.cloned.1.call-update) | async-done | bytes 3145744 | tf_op jit(solution)/shard_map/all_gather | solution.py:86
  184.3 16.5 %copy.60 = bf16[1,64,2,12288]{1,2,0,3:T(2,128)(2,1)} copy(bf16[1,64,2,12288]{3,2,1,0:T(2,128)(2,1)} %bitcast.75) | data formatting | bytes 6291456 | tf_op jit(solution)/shard_map/broadcast_in_dim | solution.py:87
  200.8 8.9 %reshape.125 = bf16[8,2,98304]{2,1,0:T(2,128)(2,1)} reshape(bf16[12288,1,2,64]{3,2,1,0:T(2,128)(2,1)} %bitcast.71) | data formatting | bytes 6291456
  209.8 80.2 %all_to_all.30 = bf16[8,2,98304]{2,1,0:T(2,128)(2,1)} all-to-all(bf16[8,2,98304]{2,1,0:T(2,128)(2,1)} %reshape.125), channel_id=1, replica_groups=mesh['batch'=8,'gx'=8,'gy'=4] {'gx'}, dimensions={0} | all-to-all | bytes 6291456 | tf_op jit(solution)/shard_map/all_to_all | solution.py:87
  290.0 8.8 %reshape.126 = bf16[12288,1,2,64]{3,2,1,0:T(2,128)(2,1)} reshape(bf16[8,2,98304]{2,1,0:T(2,128)(2,1)} %all_to_all.30) | data formatting | bytes 6291456
  298.8 10.5 %copy.72 = bf16[1,64,2,8,1536]{4,3,1,2,0:T(8,128)(2,1)} copy(bf16[1,64,2,8,1536]{1,2,4,3,0:T(2,128)(2,1)} %bitcast.72) | data formatting | bytes 6291456 | tf_op jit(solution)/shard_map/all_to_all | solution.py:87
  309.3 6.2 %fusion.14 = bf16[8,8,8,2,576]{4,2,3,0,1:T(8,128)(2,1)S(1)} fusion(bf16[1536,576]{0,1:T(8,128)(2,1)} %param.10, bf16[8,8,8,2,1536]{4,0,2,1,3:T(8,128)(2,1)} %bitcast.76), kind=kOutput, calls=%fused_computation.15 | convolution fusion | flops 1812529152 | bytes 6094848 | tf_op jit(solution)/shard_map/grtc,cd->grtd/dot_general | solution.py:88
  315.5 1.2 copy.64
  316.8 34.1 %reduce-scatter.5.cloned.1.call-done = bf16[64,2,576]{2,0,1:T(8,128)(2,1)} async-done(((bf16[512,2,576]{2,0,1:T(8,128)(2,1)}), bf16[64,2,576]{2,0,1:T(8,128)(2,1)}) %reduce-scatter.5.cloned.1.call-update) | async-done | bytes 147472 | tf_op jit(solution)/shard_map/reduce_scatter | solution.py:93
  350.9 1.8 copy.65
  (23 shorter events, 0.2 us)
Async XLA Ops:
  6.5 129.4 %copy-start = (bf16[2,2048,256]{2,1,0:T(8,128)(2,1)S(1)}, bf16[2,2048,256]{2,1,0:T(8,128)(2,1)}, u32[]{:S(2)}) copy-start(bf16[2,2048,256]{2,1,0:T(8,128)(2,1)} %param.11) | copy-start | bytes 6291460
  6.5 112.5 %reduce-scatter.3.cloned.1.call-start = ((), (), s32[]{:S(2)}) async-start(), calls=%async_computation.4 | async-start | bytes 7028736 | tf_op jit(solution)/shard_map/reduce_scatter | solution.py:66
  8.4 1.3 copy-start.1
  21.5 0.7 copy-start.2
  120.7 14.8 %all-to-all-start = ((bf16[2,8,2,1600]{3,2,0,1:T(2,128)(2,1)}), bf16[2,8,2,1600]{3,2,0,1:T(2,128)(2,1)S(1)}, u32[]{:S(2)}, u32[]{:S(2)}) async-start(bf16[2,8,2,1600]{3,2,0,1:T(2,128)(2,1)} %copy.58), calls=%async_computation.1 | async-start | bytes 212992 | tf_op jit(solution)/shard_map/all_to_all | solution.py:72
  128.2 56.1 %all-gather.2.cloned.1.call-start = ((), (), s32[]{:S(2)}) async-start(), calls=%async_computation.5 | async-start | bytes 3244032 | tf_op jit(solution)/shard_map/all_gather | solution.py:86
  135.9 1.7 copy-start.3
  138.9 212.0 %reduce-scatter.5.cloned.1.call-start = ((), (), s32[]{:S(2)}) async-start(), calls=%async_computation.6 | async-start | bytes 1474560 | tf_op jit(solution)/shard_map/reduce_scatter | solution.py:93
Sparse Core Ops, SparseCore 0:
  21.7 97.3 reduce-scatter.2
  139.0 45.2 all-gather.1
  316.9 33.9 reduce-scatter.4
where the time goes:
time: 362 us; the launch traced here: 359 us
  waiting for transfers between devices  184 us (51%)
  blocking collectives  80.2 us (22%)
  local copies, waits for them, and re-layouts  59.8 us (17%)
  between operations  13.2 us (4%)
  matrix products  13 us (4%)
  starting transfers between devices  7.53 us (2%)
    reduce_scatter x1, waiting for transfers between devices, local(): lax.psum_scatter(jnp.einsum('rgtd,dc->rgtc', arranged, joined, preferred_...  96.8 us
    all_to_all x1, blocking collectives, local(): lax.all_to_all(everyone[None], 'gx', split_axis=3, concat_axis=0, tiled=T...  80.2 us
    all_gather x1, waiting for transfers between devices, local(): everyone = lax.all_gather(attended, ('batch', 'gy'), axis=0, tiled=True)  45.4 us
    reduce_scatter x1, waiting for transfers between devices, local(): lax.psum_scatter(ordered.astype(jnp.bfloat16), 'gx', scatter_dimension=0,...  34.1 us
    unnamed x12, local copies, waits for them, and re-layouts  20.3 us
    broadcast_in_dim x1, local copies, waits for them, and re-layouts, local(): everyone[None]  16.5 us
    all_to_all x1, local copies, waits for them, and re-layouts, local(): lax.all_to_all(everyone[None], 'gx', split_axis=3, concat_axis=0, tiled=T...  10.5 us
    all_to_all x1, starting transfers between devices, local(): lax.all_to_all(summed, 'gx', split_axis=1, concat_axis=3, tiled=True)  7.48 us
  transfers between devices with their start and end apart: 4, of which 4 were waited for; matrix products, arithmetic and copies ran while one was open for 0% of the time, Pallas kernels for 0%

commit v1 on v0

v1 whole, which is shorter than its diff:
```python
import functools

import jax
import jax.numpy as jnp
import numpy as np
from jax import lax
from jax.experimental import pallas as pl
from jax.experimental.pallas import tpu as pltpu
from jax.sharding import PartitionSpec as P

MESH = pl.DeviceIdType.MESH
BF = jnp.bfloat16
F32 = jnp.float32
NX, NY, NZ = 4, 4, 8
D_LOC, COLS = 576, 1536
HD, SLOTS = 256, 2048
LEFT, RIGHT = 768, 896


def dot_nt(a, b):
    return lax.dot_general(a, b, (((1,), (1,)), ((), ())), preferred_element_type=F32)


def dot_nn(a, b):
    return lax.dot_general(a, b, (((1,), (0,)), ((), ())), preferred_element_type=F32)


def grid_of(rows, cols):
    return (
        lax.broadcasted_iota(jnp.int32, (rows, cols), 0),
        lax.broadcasted_iota(jnp.int32, (rows, cols), 1),
    )


def one_hot(hit):
    return jnp.where(hit, 1.0, 0.0).astype(BF)


def kernel(
    tok, wq, wkv, wo, ck, cv, lens, freq, out,
    vtok, vwq, vwkv, vwo, vk, vv, vfreq, xp,
    sib_s, sib_r, part0, part1, part2, part3, got0, got1, got2, got3,
    mid0, mid1, mid2, mid3, fin0, fin1, fin2, fin3,
    stack, qs, qr, ats, atr, g, zpart, zs, zr,
    ld_sem, send_sem, recv_sem,
):
    b = lax.axis_index("batch")
    z = lax.axis_index("gx")
    x = lax.axis_index("gy")
    y, c = b // 2, b % 2

    loads = {}
    for k, (name, src, dst) in enumerate([
        ("tok", tok, vtok),
        ("wq", wq, vwq),
        ("wkv", wkv, vwkv.at[pl.ds(0, 64)]),
        ("freq", freq, vfreq),
        ("k", ck, vk),
        ("v", cv, vv),
        ("wo", wo, vwo.at[pl.ds(0, D_LOC)]),
        ("wo2", wo.at[pl.ds(512, 64)], vwo.at[pl.ds(D_LOC, 64)]),
    ]):
        loads[name] = pltpu.make_async_copy(src, dst, ld_sem.at[k])
        loads[name].start()

    def at_x(o):
        return (b, z, (x + o) % NX)

    def at_y(o):
        return ((b + 2 * o) % (2 * NY), z, x)

    def at_z(o):
        return (b, (z + o) % NZ, x)

    sibling = (y * 2 + (1 - c), z, x)

    barrier = pltpu.get_barrier_semaphore()
    partners = [sibling] + [at_x(o) for o in (1, 2, 3)] + [at_y(o) for o in (1, 2, 3)]
    partners += [at_z(o) for o in range(1, NZ)]
    for partner in partners:
        pl.semaphore_signal(barrier, inc=1, device_id=partner, device_id_type=MESH)

    count = [0]
    sent = []

    def copy_to(src, dst, device):
        k = count[0]
        count[0] += 1
        copy = pltpu.make_async_remote_copy(
            src_ref=src, dst_ref=dst, send_sem=send_sem.at[k], recv_sem=recv_sem.at[k],
            device_id=device, device_id_type=MESH,
        )
        copy.start()
        sent.append(copy)
        return copy

    vwkv[64:128, :] = jnp.zeros((64, D_LOC), BF)
    r, k = grid_of(256, 256)
    perm = one_hot(
        k == (r & 1) * 128 + ((r >> 6) & 1) * 64 + ((r >> 1) & 7) * 8 + ((r >> 4) & 3) * 2 + (r >> 7)
    )
    loads["tok"].wait()
    for yy in range(NY):
        both = jnp.concatenate(
            [vtok[0, :, yy * 128:(yy + 1) * 128], vtok[1, :, yy * 128:(yy + 1) * 128]], axis=1
        )
        rows = dot_nt(perm, both).astype(BF)
        for s in range(2):
            for cc in range(2):
                at = (s * 2 + cc) * 64
                xp[s, cc, yy * 64:(yy + 1) * 64, :] = rows[at:at + 64]
    pl.semaphore_wait(barrier, len(partners))
    loads["wq"].wait()
    loads["wkv"].wait()

    parts, gots = (part0, part1, part2, part3), (got0, got1, got2, got3)
    mids, fins = (mid0, mid1, mid2, mid3), (fin0, fin1, fin2, fin3)
    first_x = (True, False, False, True)

    def project(s, side, core):
        rows = xp[s, core]
        if side == 0:
            return dot_nn(rows, vwq[:, 0:LEFT])
        return jnp.concatenate([dot_nn(rows, vwq[:, LEFT:COLS]), dot_nt(rows, vwkv[...])], axis=1)

    def width(side):
        return LEFT if side == 0 else RIGHT

    def cols_of(side):
        return pl.ds(0, LEFT) if side == 0 else pl.ds(LEFT, RIGHT)

    stage1 = {}

    def start_unit(u):
        s, side = divmod(u, 2)
        cols = cols_of(side)
        sib_s[s, :, cols] = project(s, side, 1 - c).astype(BF)
        swap = copy_to(sib_s.at[s, :, cols], sib_r.at[s, :, cols], sibling)
        own = project(s, side, c)
        swap.wait_recv()
        total = (own + sib_r[s, :, cols].astype(F32)).astype(BF)
        for yy in range(NY):
            for xx in range(NX):
                at = (yy * NX + xx) * 16
                lead = (xx, yy) if first_x[u] else (yy, xx)
                parts[u][lead[0], lead[1]] = total[at:at + 16]
        me, to = (x, at_x) if first_x[u] else (y, at_y)
        stage1[u] = [
            copy_to(parts[u].at[(me + o) % 4], gots[u].at[o - 1], to(o)) for o in (2, 1, 3)
        ]

    stage2 = {}

    def middle_unit(u):
        me, to, other = (x, at_y, y) if first_x[u] else (y, at_x, x)
        for copy in stage1[u]:
            copy.wait_recv()
        total = parts[u][me].astype(F32)
        for o in range(3):
            total = total + gots[u][o].astype(F32)
        mids[u][...] = total.astype(BF)
        stage2[u] = [copy_to(mids[u].at[(other + o) % 4], fins[u].at[o - 1], to(o)) for o in (2, 1, 3)]

    def finish_unit(u):
        other = y if first_x[u] else x
        for copy in stage2[u]:
            copy.wait_recv()
        total = mids[u][other].astype(F32)
        for o in range(3):
            total = total + fins[u][o].astype(F32)
        return total.astype(BF)

    r, k = grid_of(128, 128)
    slot = r & 15
    to_groups = one_hot((slot < 14) & (k == (slot >> 1) * 16 + (r >> 4) * 2 + (slot & 1)))
    r, k = grid_of(128, 256)
    place = one_hot((r < 64) & (k == r + (z % 4) * 64))

    exchange = {}

    def send_queries(s):
        left = finish_unit(2 * s)
        right = finish_unit(2 * s + 1)
        for h in range(3):
            stack[s, h * 16:(h + 1) * 16] = left[:, h * HD:(h + 1) * HD]
            stack[s, (h + 3) * 16:(h + 4) * 16] = right[:, h * HD:(h + 1) * HD]
        stack[s, 96:112] = dot_nn(right[:, LEFT:RIGHT], place).astype(BF)
        stack[s, 112:128] = jnp.zeros((16, HD), BF)
        grouped = dot_nn(to_groups, stack[s]).astype(BF)
        for zz in range(NZ):
            qs[s, zz] = grouped[zz * 16:(zz + 1) * 16]
        exchange[s] = [
            copy_to(qs.at[s, (z + o) % NZ], qr.at[s, z], at_z(o)) for o in (4, 3, 5, 2, 6, 1, 7)
        ]
        qr[s, z] = qs[s, z]

    loads["freq"].wait()
    r, _ = grid_of(8, 128)
    length = jnp.where((r & 2) == 0, lens[0], lens[1])
    angle = (length + (r & 1)).astype(F32) * vfreq[...]
    cosine, sine = jnp.cos(angle), jnp.sin(angle)

    r, k = grid_of(128, 128)
    pick_key = one_hot((r < 2) & ((k & 15) == 12 + r) & ((k >> 4) < 4))
    pick_value = one_hot((r < 2) & ((k & 15) == 12 + r) & ((k >> 4) >= 4))
    odd = (r & 1) == 1
    causal = k <= (r & 1)

    def attention(s):
        for copy in exchange[s]:
            copy.wait_recv()
        raw = qr[s].reshape(128, HD)
        cos_rows = jnp.where(odd, cosine[2 * s + 1:2 * s + 2], cosine[2 * s:2 * s + 1])
        sin_rows = jnp.where(odd, sine[2 * s + 1:2 * s + 2], sine[2 * s:2 * s + 1])

        def rotate(values):
            u, w = values[:, :128], values[:, 128:]
            return jnp.concatenate(
                [u * cos_rows - w * sin_rows, w * cos_rows + u * sin_rows], axis=1
            ).astype(BF)

        queries = rotate(raw.astype(F32))
        new_keys = rotate(dot_nn(pick_key, raw))
        new_values = dot_nn(pick_value, raw).astype(BF)
        if s == 0:
            loads["k"].wait()
        scale = 1.0 / HD**0.5
        cached = dot_nt(queries, vk[s]) * scale
        _, column = grid_of(128, SLOTS)
        cached = jnp.where(column < lens[s], cached, -1e30)
        fresh = jnp.where(causal, dot_nt(queries, new_keys) * scale, -1e30)
        highest = jnp.maximum(cached.max(-1, keepdims=True), fresh.max(-1, keepdims=True))
        cached = jnp.exp(cached - highest)
        fresh = jnp.exp(fresh - highest)
        denom = cached.sum(-1, keepdims=True) + fresh.sum(-1, keepdims=True)
        if s == 0:
            loads["v"].wait()
        result = dot_nn(cached.astype(BF), vv[s]) + dot_nn(fresh.astype(BF), new_values)
        result = (result / denom).astype(BF)
        for zz in range(NZ):
            ats[s, zz] = result[zz * 16:(zz + 1) * 16]
        exchange[s] = [
            copy_to(ats.at[s, (z + o) % NZ], atr.at[s, z], at_z(o)) for o in (4, 3, 5, 2, 6, 1, 7)
        ]
        atr[s, z] = ats[s, z]

    halves = (pl.ds(0, COLS // 2), pl.ds(COLS // 2, COLS // 2))
    to_heads = one_hot((r < 96) & (k == ((r >> 1) & 7) * 16 + (r >> 4) * 2 + (r & 1)))
    gather1, gather2, siblings = {}, {}, {0: [], 1: []}

    def gather_start(s):
        for copy in exchange[s]:
            copy.wait_recv()
        heads = dot_nn(to_heads, atr[s].reshape(128, HD)).astype(BF)
        for h in range(6):
            g[s, y, c, x, :, h * HD:(h + 1) * HD] = heads[h * 16:(h + 1) * 16]
        mine_l = g.at[s, y, c, x, :, halves[0]]
        mine_r = g.at[s, y, c, x, :, halves[1]]
        gather1[s] = []
        for o in (2, 1, 3):
            gather1[s].append(copy_to(mine_l, mine_l, at_x(o)))
            gather1[s].append(copy_to(mine_r, mine_r, at_y(o)))
        siblings[s].append(copy_to(g.at[s, y, c, x], g.at[s, y, c, x], sibling))

    def gather_middle(s):
        for copy in gather1[s]:
            copy.wait_recv()
        block_l = g.at[s, y, c, :, :, halves[0]]
        block_r = g.at[s, :, c, x, :, halves[1]]
        gather2[s] = []
        for o in (2, 1, 3):
            gather2[s].append((copy_to(block_l, block_l, at_y(o)), copy_to(block_r, block_r, at_x(o)), o))
        for o in (1, 2, 3):
            piece = g.at[s, y, c, (x + o) % NX, :, halves[0]]
            siblings[s].append(copy_to(piece, piece, sibling))
            piece = g.at[s, (y + o) % NY, c, x, :, halves[1]]
            siblings[s].append(copy_to(piece, piece, sibling))

    def gather_end(s):
        for from_y, from_x, o in gather2[s]:
            from_y.wait_recv()
            block = g.at[s, (y + 4 - o) % NY, c, :, :, halves[0]]
            siblings[s].append(copy_to(block, block, sibling))
            from_x.wait_recv()
            block = g.at[s, :, c, (x + 4 - o) % NX, :, halves[1]]
            siblings[s].append(copy_to(block, block, sibling))
        for copy in siblings[s]:
            copy.wait_recv()

    low = lax.broadcasted_iota(jnp.int32, (32, 128), 1) < 64

    def output_terms(s):
        if s == 0:
            loads["wo"].wait()
            loads["wo2"].wait()
        terms = dot_nt(g[s].reshape(512, COLS), vwo[...])
        for bb in range(8):
            mine = terms[bb * 64:(bb + 1) * 64]
            for cb in range(4):
                for half in range(2):
                    zpart[s, bb, 2 * cb + half] = mine[half * 32:(half + 1) * 32, cb * 128:(cb + 1) * 128]
            zpart[s, bb, 8] = jnp.where(low, mine[:32, 512:640], mine[32:, 512:640])

    ring = {}

    def ring_step(s, step):
        if step == 0:
            far = zpart[s, (z + 4) % NZ].astype(BF)
            zs[s, 0, 0, 0:5] = far[0:5]
            zs[s, 1, 0, 0:4] = far[5:9]
            ring[s] = [
                copy_to(zs.at[s, 0, 0, pl.ds(0, 5)], zr.at[s, 0, 0, pl.ds(0, 5)], at_z(1)),
                copy_to(zs.at[s, 1, 0, pl.ds(0, 4)], zr.at[s, 1, 0, pl.ds(0, 4)], at_z(7)),
            ]
            return
        copies = []
        for way in range(2):
            ring[s][way].wait_recv()
            dest = (z + 4 - step) % NZ if way == 0 else (z + 4 + step) % NZ
            own = zpart[s, dest]
            if step == 1:
                if way == 0:
                    zs[s, 0, 1, 0:5] = (own[0:5] + zr[s, 0, 0, 0:5].astype(F32)).astype(BF)
                    zs[s, 0, 1, 5:9] = own[5:9].astype(BF)
                else:
                    zs[s, 1, 1, 0:5] = own[0:5].astype(BF)
                    zs[s, 1, 1, 5:9] = (own[5:9] + zr[s, 1, 0, 0:4].astype(F32)).astype(BF)
            else:
                zs[s, way, step] = (own + zr[s, way, step - 1].astype(F32)).astype(BF)
            copies.append(copy_to(zs.at[s, way, step], zr.at[s, way, step], at_z(1 if way == 0 else 7)))
        ring[s] = copies

    def ring_end(s):
        for copy in ring[s]:
            copy.wait_recv()
        total = zpart[s, z] + zr[s, 0, 3].astype(F32) + zr[s, 1, 3].astype(F32)
        return total.astype(BF)

    for u in range(4):
        start_unit(u)
    for u in (0, 1):
        middle_unit(u)
    send_queries(0)
    for u in (2, 3):
        middle_unit(u)
    attention(0)
    send_queries(1)
    gather_start(0)
    attention(1)
    gather_middle(0)
    gather_start(1)
    gather_end(0)
    output_terms(0)
    ring_step(0, 0)
    gather_middle(1)
    ring_step(0, 1)
    gather_end(1)
    output_terms(1)
    ring_step(1, 0)
    ring_step(0, 2)
    ring_step(1, 1)
    ring_step(0, 3)
    ring_step(1, 2)
    first = ring_end(0)
    ring_step(1, 3)
    second = ring_end(1)

    from_row = (k == ((r >> 1) & 1) * 64 + ((r >> 2) & 3) * 16 + (r >> 4) * 2 + (r & 1))
    to_rows = one_hot(from_row)
    for cb in range(4):
        both = jnp.concatenate(
            [first[2 * cb:2 * cb + 2].reshape(64, 128), second[2 * cb:2 * cb + 2].reshape(64, 128)], axis=0
        )
        out[:, cb * 128:(cb + 1) * 128] = dot_nn(to_rows, both).astype(BF)
    tails = jnp.concatenate([first[8], first[8], second[8], second[8]], axis=0)
    in_low = one_hot(from_row & ((k & 32) == 0))
    in_high = one_hot(from_row & ((k & 32) != 0))
    tail = dot_nn(in_low, tails) + pltpu.roll(dot_nn(in_high, tails), 64, 1)
    out[:, 512:576] = tail[:, :64].astype(BF)

    for copy in sent:
        copy.wait_send()


def local(tokens, w_query, w_keyval, w_out, cache_keys, cache_values, lengths):
    freqs = 10000.0 ** (-(np.arange(128, dtype=np.float32) * np.float32(2.0) / np.float32(256)))
    freqs = jnp.asarray(np.broadcast_to(freqs.astype(np.float32)[None], (8, 128)))
    vm = pltpu.VMEM
    units = (LEFT, RIGHT, LEFT, RIGHT)
    scratch = [
        vm((2, D_LOC, 512), BF), vm((D_LOC, COLS), BF), vm((128, D_LOC), BF), vm((640, COLS), BF),
        vm((2, SLOTS, HD), BF), vm((2, SLOTS, HD), BF), vm((8, 128), F32), vm((2, 2, 256, D_LOC), BF),
        vm((2, 256, LEFT + RIGHT), BF), vm((2, 256, LEFT + RIGHT), BF),
        *[vm((4, 4, 16, w), BF) for w in units],
        *[vm((3, 4, 16, w), BF) for w in units],
        *[vm((4, 16, w), BF) for w in units],
        *[vm((3, 16, w), BF) for w in units],
        vm((2, 128, HD), BF),
        *[vm((2, NZ, 16, HD), BF) for _ in range(4)],
        vm((2, NY, 2, NX, 16, COLS), BF),
        vm((2, NZ, 9, 32, 128), F32),
        vm((2, 2, 4, 9, 32, 128), BF), vm((2, 2, 4, 9, 32, 128), BF),
        pltpu.SemaphoreType.DMA((8,)), pltpu.SemaphoreType.DMA((160,)), pltpu.SemaphoreType.DMA((160,)),
    ]
    hbm = pl.BlockSpec(memory_space=pl.ANY)
    result = pl.pallas_call(
        kernel,
        out_shape=jax.ShapeDtypeStruct((128, D_LOC), BF),
        in_specs=[hbm] * 6 + [pl.BlockSpec(memory_space=pltpu.SMEM), hbm],
        out_specs=pl.BlockSpec(memory_space=pltpu.VMEM),
        scratch_shapes=scratch,
        compiler_params=pltpu.CompilerParams(
            collective_id=0, has_side_effects=True, vmem_limit_bytes=56 * 2**20
        ),
        cost_estimate=pl.CostEstimate(flops=4 * 10**9, bytes_accessed=10**7, transcendentals=10**6),
        name="layer",
    )(
        tokens.transpose(1, 2, 0), w_query, w_keyval.T, w_out.T, cache_keys, cache_values, lengths, freqs
    )
    return result.reshape(64, 2, D_LOC)


def solution(mesh):
    placed = (
        P(None, None, ("batch", "gy")),
        P(("batch", "gy"), "gx"),
        P(("batch", "gy"), "gx"),
        P("gx", ("batch", "gy")),
        P(("batch", "gx", "gy"), None, None),
        P(("batch", "gx", "gy"), None, None),
        P(("batch", "gx", "gy")),
    )
    return jax.shard_map(
        local, mesh=mesh, in_specs=placed, out_specs=P("gx", None, ("batch", "gy")), check_vma=False
    )
```

time: 362 us -> 82.9 us (0.23)
  waiting for transfers between devices: 184 us -> 0 us
  blocking collectives: 80.2 us -> 0 us
  Pallas kernels: 0 us -> 79.9 us
  local copies, waits for them, and re-layouts: 59.8 us -> 2.9 us
  between operations: 13.2 us -> 0.01 us
  matrix products: 13 us -> 0 us
  starting transfers between devices: 7.53 us -> 0 us
    reduce_scatter x2 -> x0, waiting for transfers between devices: 131 us -> none  [the longest x1 96.8 us: local(): lax.psum_scatter(jnp.einsum('rgtd,dc->rgtc', arranged, joined, preferred_...]
    all_to_all x1 -> x0, blocking collectives: 80.2 us -> none  [local(): lax.all_to_all(everyone[None], 'gx', split_axis=3, concat_axis=0, tiled=T...]
    pallas_call x0 -> x1, Pallas kernels: none -> 79.9 us  [local(): pl.pallas_call(kernel, out_shape=jax.ShapeDtypeStruct((128, D_LOC), BF),...]
    all_gather x1 -> x0, waiting for transfers between devices: 45.4 us -> none  [local(): everyone = lax.all_gather(attended, ('batch', 'gy'), axis=0, tiled=True)]
    unnamed x12 -> x0, local copies, waits for them, and re-layouts: 20.3 us -> none
    broadcast_in_dim x1 -> x0, local copies, waits for them, and re-layouts: 16.5 us -> none  [local(): everyone[None]]
    dot_general x6 -> x0, matrix products: 13 us -> none  [the longest x1 6.23 us: local(): jnp.einsum('grtc,cd->grtd', grouped, w_out, preferred_element_type=jnp.fl...]
    all_to_all x2 -> x0, local copies, waits for them, and re-layouts: 10.5 us -> none  [the longest x1 10.5 us: local(): lax.all_to_all(everyone[None], 'gx', split_axis=3, concat_axis=0, tiled=T...]
  transfers between devices with their start and end apart: 4 -> 0, of which waited for: 4 -> 0; matrix products, arithmetic and copies ran while one was open for 0% -> 0% of each run, Pallas kernels for 0% -> 0%
where the time goes in v1:
time: 82.9 us; the launch traced here: 82.8 us
  Pallas kernels  79.9 us (96%)
  local copies, waits for them, and re-layouts  2.9 us (3%)
    pallas_call x1, Pallas kernels, local(): pl.pallas_call(kernel, out_shape=jax.ShapeDtypeStruct((128, D_LOC), BF),...  79.9 us

profile of v1, /device:TPU:32, one launch (start us, length us, event | category | flops | bytes accessed | tf_op | source)
XLA Modules:
  0.0 82.8 jit_solution(15064498708822033064)
XLA Ops:
  0.0 1.2 %jit_solution_.3.freq = f32[8,128]{1,0:T(8,128)} broadcast(f32[128]{0:T(128)} %constant.2.clone), dimensions={1} | broadcast | bytes 4608 | tf_op jit(solution)
  1.2 79.9 %layer.1 = bf16[128,576]{1,0:T(8,128)(2,1)} custom-call(bf16[2,576,512]{2,1,0:T(8,128)(2,1)} %bitcast.4, bf16[576,1536]{1,0:T(8,128)(2,1)} %wq.1, bf16[64,576]{1,0:T(8,128)(2,1)} %bitcast.5, bf16[576,1536]{1,0:T(8,128)(2,1)} %bitcast.3, bf16[2,2048,256]{2,1,0:T(8,128)(2,1)} %ck.1, bf16[2,2048,256]{2,1,0:T(8,128)(2,1)} %cv.1, s32[2]{0:T(128)} %lens.1, ...), custom_call_target="tpu_custom_call" | custom-call | flops 4000000000 | bytes 10000000 | tf_op jit(solution)/shard_map/layer/pallas_call | solution.py:406
  81.2 1.7 %reshape.3 = bf16[64,2,576]{2,1,0:T(2,128)(2,1)} reshape(bf16[128,576]{1,0:T(8,128)(2,1)} %layer.1) | data formatting | bytes 294912 | tf_op jit(solution)/shard_map/reshape | solution.py:420

commit v2 on v1

v2 whole, which is shorter than its diff:
```python
import functools

import jax
import jax.numpy as jnp
import numpy as np
from jax import lax
from jax.experimental import pallas as pl
from jax.experimental.pallas import tpu as pltpu
from jax.sharding import PartitionSpec as P

MESH = pl.DeviceIdType.MESH
BF = jnp.bfloat16
F32 = jnp.float32
NX, NY, NZ = 4, 4, 8
D_LOC, COLS = 576, 1536
HD, SLOTS = 256, 2048
SEND_SLOTS = 32
SWAP, STAGE1, STAGE2, QUERIES, RESULTS, GATHER1, FORWARD, GATHER2, RING = 0, 4, 8, 12, 14, 16, 18, 20, 32
LEFT, RIGHT = 768, 896


def dot_nt(a, b):
    return lax.dot_general(a, b, (((1,), (1,)), ((), ())), preferred_element_type=F32)


def dot_nn(a, b):
    return lax.dot_general(a, b, (((1,), (0,)), ((), ())), preferred_element_type=F32)


def grid_of(rows, cols):
    return (
        lax.broadcasted_iota(jnp.int32, (rows, cols), 0),
        lax.broadcasted_iota(jnp.int32, (rows, cols), 1),
    )


def one_hot(hit):
    return jnp.where(hit, 1.0, 0.0).astype(BF)


def kernel(
    tok, wq, wkv, wo, ck, cv, lens_in, out,
    vtok, vwq, vwkv, vwo, vk, vv, lens, xp,
    sib_s, sib_r, part0, part1, part2, part3, got0, got1, got2, got3,
    mid0, mid1, mid2, mid3, fin0, fin1, fin2, fin3,
    stack, qs, qr, ats, atr, g, zpart, zs, zr,
    ld_sem, send_sem, recv_sem,
):
    b = lax.axis_index("batch")
    z = lax.axis_index("gx")
    x = lax.axis_index("gy")
    y, c = b // 2, b % 2

    loads = {}
    for k, (name, src, dst) in enumerate([
        ("tok", tok, vtok),
        ("wq", wq, vwq),
        ("wkv", wkv, vwkv.at[pl.ds(0, 64)]),
        ("lens", lens_in, lens),
        ("k", ck, vk),
        ("v", cv, vv),
        ("wo", wo, vwo.at[pl.ds(0, D_LOC)]),
        ("wo2", wo.at[pl.ds(512, 64)], vwo.at[pl.ds(D_LOC, 64)]),
    ]):
        loads[name] = pltpu.make_async_copy(src, dst, ld_sem.at[k])
        loads[name].start()

    def at_x(o):
        return (b, z, (x + o) % NX)

    def at_y(o):
        return ((b + 2 * o) % (2 * NY), z, x)

    def at_z(o):
        return (b, (z + o) % NZ, x)

    sibling = (y * 2 + (1 - c), z, x)

    barrier = pltpu.get_barrier_semaphore()
    partners = [sibling] + [at_x(o) for o in (1, 2, 3)] + [at_y(o) for o in (1, 2, 3)]
    partners += [at_z(o) for o in range(1, NZ)]
    for partner in partners:
        pl.semaphore_signal(barrier, inc=1, device_id=partner, device_id_type=MESH)

    slots = [None] * SEND_SLOTS
    count = [0]

    def copy_to(src, dst, device, sem):
        k = count[0] % SEND_SLOTS
        count[0] += 1
        if slots[k] is not None:
            slots[k].wait_send()
        copy = pltpu.make_async_remote_copy(
            src_ref=src, dst_ref=dst, send_sem=send_sem.at[k], recv_sem=recv_sem.at[sem],
            device_id=device, device_id_type=MESH,
        )
        copy.start()
        slots[k] = copy

    def arrived(ref, sem):
        pltpu.make_async_copy(ref, ref, recv_sem.at[sem]).wait()

    vwkv[64:128, :] = jnp.zeros((64, D_LOC), BF)
    r, k = grid_of(256, 256)
    perm = one_hot(
        k == (r & 1) * 128 + ((r >> 6) & 1) * 64 + ((r >> 1) & 7) * 8 + ((r >> 4) & 3) * 2 + (r >> 7)
    )
    loads["tok"].wait()
    for yy in range(NY):
        both = jnp.concatenate(
            [vtok[0, :, yy * 128:(yy + 1) * 128], vtok[1, :, yy * 128:(yy + 1) * 128]], axis=1
        )
        rows = dot_nt(perm, both).astype(BF)
        for s in range(2):
            for cc in range(2):
                at = (s * 2 + cc) * 64
                xp[s, cc, yy * 64:(yy + 1) * 64, :] = rows[at:at + 64]
    loads["wq"].wait()
    loads["wkv"].wait()

    parts, gots = (part0, part1, part2, part3), (got0, got1, got2, got3)
    mids, fins = (mid0, mid1, mid2, mid3), (fin0, fin1, fin2, fin3)
    first_x = (True, False, False, True)

    def project(s, side, core):
        rows = xp[s, core]
        if side == 0:
            return dot_nn(rows, vwq[:, 0:LEFT])
        return jnp.concatenate([dot_nn(rows, vwq[:, LEFT:COLS]), dot_nt(rows, vwkv[...])], axis=1)

    def width(side):
        return LEFT if side == 0 else RIGHT

    def cols_of(side):
        return pl.ds(0, LEFT) if side == 0 else pl.ds(LEFT, RIGHT)

    def swap_unit(u):
        s, side = divmod(u, 2)
        cols = cols_of(side)
        sib_s[s, :, cols] = project(s, side, 1 - c).astype(BF)
        if u == 0:
            pl.semaphore_wait(barrier, len(partners))
        copy_to(sib_s.at[s, :, cols], sib_r.at[s, :, cols], sibling, SWAP + u)

    def start_unit(u):
        s, side = divmod(u, 2)
        cols = cols_of(side)
        own = project(s, side, c)
        arrived(sib_r.at[s, :, cols], SWAP + u)
        total = (own + sib_r[s, :, cols].astype(F32)).astype(BF)
        for yy in range(NY):
            for xx in range(NX):
                at = (yy * NX + xx) * 16
                lead = (xx, yy) if first_x[u] else (yy, xx)
                parts[u][lead[0], lead[1]] = total[at:at + 16]
        me, to = (x, at_x) if first_x[u] else (y, at_y)
        for o in (2, 1, 3):
            copy_to(parts[u].at[(me + o) % 4], gots[u].at[o - 1], to(o), STAGE1 + u)

    def middle_unit(u):
        me, to, other = (x, at_y, y) if first_x[u] else (y, at_x, x)
        arrived(gots[u], STAGE1 + u)
        total = parts[u][me].astype(F32)
        for o in range(3):
            total = total + gots[u][o].astype(F32)
        mids[u][...] = total.astype(BF)
        for o in (2, 1, 3):
            copy_to(mids[u].at[(other + o) % 4], fins[u].at[o - 1], to(o), STAGE2 + u)

    def finish_unit(u):
        other = y if first_x[u] else x
        arrived(fins[u], STAGE2 + u)
        total = mids[u][other].astype(F32)
        for o in range(3):
            total = total + fins[u][o].astype(F32)
        return total.astype(BF)

    r, k = grid_of(128, 128)
    slot = r & 15
    to_groups = one_hot((slot < 14) & (k == (slot >> 1) * 16 + (r >> 4) * 2 + (slot & 1)))
    r, k = grid_of(128, 256)
    place = one_hot((r < 64) & (k == r + (z % 4) * 64))

    def send_queries(s):
        left = finish_unit(2 * s)
        right = finish_unit(2 * s + 1)
        for h in range(3):
            stack[s, h * 16:(h + 1) * 16] = left[:, h * HD:(h + 1) * HD]
            stack[s, (h + 3) * 16:(h + 4) * 16] = right[:, h * HD:(h + 1) * HD]
        stack[s, 96:112] = dot_nn(right[:, LEFT:RIGHT], place).astype(BF)
        stack[s, 112:128] = jnp.zeros((16, HD), BF)
        grouped = dot_nn(to_groups, stack[s]).astype(BF)
        for zz in range(NZ):
            qs[s, zz] = grouped[zz * 16:(zz + 1) * 16]
        for o in (4, 3, 5, 2, 6, 1, 7):
            copy_to(qs.at[s, (z + o) % NZ], qr.at[s, z], at_z(o), QUERIES + s)
        qr[s, z] = qs[s, z]

    loads["lens"].wait()
    r, k = grid_of(8, 128)
    freqs = jnp.exp(k.astype(F32) * (-np.log(10000.0) / 128))
    length = jnp.where((r & 2) == 0, lens[0], lens[1])
    angle = (length + (r & 1)).astype(F32) * freqs
    cosine, sine = jnp.cos(angle), jnp.sin(angle)

    r, k = grid_of(128, 128)
    pick_key = one_hot((r < 2) & ((k & 15) == 12 + r) & ((k >> 4) < 4))
    pick_value = one_hot((r < 2) & ((k & 15) == 12 + r) & ((k >> 4) >= 4))
    odd = (r & 1) == 1
    causal = k <= (r & 1)

    def attention(s):
        arrived(qr.at[s, pl.ds(0, NZ - 1)], QUERIES + s)
        raw = qr[s].reshape(128, HD)
        cos_rows = jnp.where(odd, cosine[2 * s + 1:2 * s + 2], cosine[2 * s:2 * s + 1])
        sin_rows = jnp.where(odd, sine[2 * s + 1:2 * s + 2], sine[2 * s:2 * s + 1])

        def rotate(values):
            u, w = values[:, :128], values[:, 128:]
            return jnp.concatenate(
                [u * cos_rows - w * sin_rows, w * cos_rows + u * sin_rows], axis=1
            ).astype(BF)

        queries = rotate(raw.astype(F32))
        new_keys = rotate(dot_nn(pick_key, raw))
        new_values = dot_nn(pick_value, raw).astype(BF)
        if s == 0:
            loads["k"].wait()
        scale = 1.0 / HD**0.5
        cached = dot_nt(queries, vk[s]) * scale
        _, column = grid_of(128, SLOTS)
        cached = jnp.where(column < lens[s], cached, -1e30)
        fresh = jnp.where(causal, dot_nt(queries, new_keys) * scale, -1e30)
        highest = jnp.maximum(cached.max(-1, keepdims=True), fresh.max(-1, keepdims=True))
        cached = jnp.exp(cached - highest)
        fresh = jnp.exp(fresh - highest)
        denom = cached.sum(-1, keepdims=True) + fresh.sum(-1, keepdims=True)
        if s == 0:
            loads["v"].wait()
        result = dot_nn(cached.astype(BF), vv[s]) + dot_nn(fresh.astype(BF), new_values)
        result = (result / denom).astype(BF)
        for zz in range(NZ):
            ats[s, zz] = result[zz * 16:(zz + 1) * 16]
        for o in (4, 3, 5, 2, 6, 1, 7):
            copy_to(ats.at[s, (z + o) % NZ], atr.at[s, z], at_z(o), RESULTS + s)
        atr[s, z] = ats[s, z]

    halves = (pl.ds(0, COLS // 2), pl.ds(COLS // 2, COLS // 2))
    to_heads = one_hot((r < 96) & (k == ((r >> 1) & 7) * 16 + (r >> 4) * 2 + (r & 1)))

    def gather_start(s):
        arrived(atr.at[s, pl.ds(0, NZ - 1)], RESULTS + s)
        heads = dot_nn(to_heads, atr[s].reshape(128, HD)).astype(BF)
        for h in range(6):
            g[s, y, c, x, :, h * HD:(h + 1) * HD] = heads[h * 16:(h + 1) * 16]
        mine_l = g.at[s, y, c, x, :, halves[0]]
        mine_r = g.at[s, y, c, x, :, halves[1]]
        for o in (2, 1, 3):
            copy_to(mine_l, mine_l, at_x(o), GATHER1 + s)
            copy_to(mine_r, mine_r, at_y(o), GATHER1 + s)
        copy_to(g.at[s, y, c, x], g.at[s, y, c, x], sibling, FORWARD + s)

    def gather_middle(s):
        arrived(g.at[s, 0, 0, pl.ds(0, 3)], GATHER1 + s)
        block_l = g.at[s, y, c, :, :, halves[0]]
        block_r = g.at[s, :, c, x, :, halves[1]]
        for o in (2, 1, 3):
            copy_to(block_l, block_l, at_y(o), GATHER2 + s * 6 + o - 1)
            copy_to(block_r, block_r, at_x(o), GATHER2 + s * 6 + o + 2)
        for o in (1, 2, 3):
            piece = g.at[s, y, c, (x + o) % NX, :, halves[0]]
            copy_to(piece, piece, sibling, FORWARD + s)
            piece = g.at[s, (y + o) % NY, c, x, :, halves[1]]
            copy_to(piece, piece, sibling, FORWARD + s)

    def gather_end(s):
        for o in (1, 3, 2):
            block = g.at[s, (y + 4 - o) % NY, c, :, :, halves[0]]
            arrived(block, GATHER2 + s * 6 + o - 1)
            copy_to(block, block, sibling, FORWARD + s)
            block = g.at[s, :, c, (x + 4 - o) % NX, :, halves[1]]
            arrived(block, GATHER2 + s * 6 + o + 2)
            copy_to(block, block, sibling, FORWARD + s)

    low = lax.broadcasted_iota(jnp.int32, (32, 128), 1) < 64

    def output_terms(s, core):
        if core == 0:
            if s == 0:
                loads["wo"].wait()
                loads["wo2"].wait()
        else:
            arrived(g.at[s, :, 1 - c], FORWARD + s)
        core = c if core == 0 else 1 - c
        terms = dot_nt(g[s, :, core].reshape(256, COLS), vwo[...])
        for yy in range(NY):
            mine = terms[yy * 64:(yy + 1) * 64]
            for cb in range(4):
                for half in range(2):
                    zpart[s, yy, core, 2 * cb + half] = mine[
                        half * 32:(half + 1) * 32, cb * 128:(cb + 1) * 128
                    ]
            zpart[s, yy, core, 8] = jnp.where(low, mine[:32, 512:640], mine[32:, 512:640])

    ends = {}
    pieces = (pl.ds(0, 5), pl.ds(5, 4))

    def ring_sem(s, way, step, sub):
        return RING + ((s * 2 + way) * 4 + step) * 2 + sub

    def ring_add(s, way, step, sub, first):
        dest = (z + 4 - step) % NZ if way == 0 else (z + 4 + step) % NZ
        total = zpart[s, dest // 2, dest % 2, pieces[sub]]
        if not first:
            arrived(zr.at[s, way, step - 1, pieces[sub]], ring_sem(s, way, step - 1, sub))
            total = total + zr[s, way, step - 1, pieces[sub]].astype(F32)
        zs[s, way, step, pieces[sub]] = total.astype(BF)
        copy_to(
            zs.at[s, way, step, pieces[sub]], zr.at[s, way, step, pieces[sub]],
            at_z(1 if way == 0 else 7), ring_sem(s, way, step, sub),
        )

    def ring_start(s):
        for way in range(2):
            ring_add(s, way, 0, way, True)
        for way in range(2):
            ring_add(s, way, 1, 1 - way, True)

    def ring_step(s, step, late):
        for way in range(2):
            ring_add(s, way, step, way if late else 1 - way, False)

    def ring_end(s):
        for way in range(2):
            for sub in range(2):
                arrived(zr.at[s, way, 3, pieces[sub]], ring_sem(s, way, 3, sub))
        total = zpart[s, z // 2, z % 2] + zr[s, 0, 3].astype(F32) + zr[s, 1, 3].astype(F32)
        ends[s] = total.astype(BF)

    steps = [
        (swap_unit, 0), (swap_unit, 1), (start_unit, 0), (start_unit, 1),
        (swap_unit, 2), (swap_unit, 3), (start_unit, 2), (start_unit, 3),
        (middle_unit, 0), (middle_unit, 1), (middle_unit, 2), (middle_unit, 3),
        (send_queries, 0), (send_queries, 1), (attention, 0), (attention, 1),
        (gather_start, 0), (gather_start, 1), (gather_middle, 0), (gather_middle, 1),
        (gather_end, 0), (output_terms, 0, 0), (output_terms, 0, 1), (ring_start, 0),
        (gather_end, 1), (output_terms, 1, 0), (output_terms, 1, 1), (ring_start, 1),
        (ring_step, 0, 1, True), (ring_step, 0, 2, False),
        (ring_step, 1, 1, True), (ring_step, 1, 2, False),
        (ring_step, 0, 2, True), (ring_step, 0, 3, False),
        (ring_step, 1, 2, True), (ring_step, 1, 3, False),
        (ring_step, 0, 3, True), (ring_step, 1, 3, True),
        (ring_end, 0), (ring_end, 1),
    ]
    for function, *arguments in steps:
        function(*arguments)
    first, second = ends[0], ends[1]

    from_row = (k == ((r >> 1) & 1) * 64 + ((r >> 2) & 3) * 16 + (r >> 4) * 2 + (r & 1))
    to_rows = one_hot(from_row)
    for cb in range(4):
        both = jnp.concatenate(
            [first[2 * cb:2 * cb + 2].reshape(64, 128), second[2 * cb:2 * cb + 2].reshape(64, 128)], axis=0
        )
        out[:, cb * 128:(cb + 1) * 128] = dot_nn(to_rows, both).astype(BF)
    tails = jnp.concatenate([first[8], first[8], second[8], second[8]], axis=0)
    in_low = one_hot(from_row & ((k & 32) == 0))
    in_high = one_hot(from_row & ((k & 32) != 0))
    tail = dot_nn(in_low, tails) + pltpu.roll(dot_nn(in_high, tails), 64, 1)
    out[:, 512:576] = tail[:, :64].astype(BF)

    for copy in slots:
        copy.wait_send()


def local(tokens, w_query, w_keyval, w_out, cache_keys, cache_values, lengths):
    vm = pltpu.VMEM
    units = (LEFT, RIGHT, LEFT, RIGHT)
    scratch = [
        vm((2, D_LOC, 512), BF), vm((D_LOC, COLS), BF), vm((128, D_LOC), BF), vm((640, COLS), BF),
        vm((2, SLOTS, HD), BF), vm((2, SLOTS, HD), BF), pltpu.SMEM((2,), jnp.int32), vm((2, 2, 256, D_LOC), BF),
        vm((2, 256, LEFT + RIGHT), BF), vm((2, 256, LEFT + RIGHT), BF),
        *[vm((4, 4, 16, w), BF) for w in units],
        *[vm((3, 4, 16, w), BF) for w in units],
        *[vm((4, 16, w), BF) for w in units],
        *[vm((3, 16, w), BF) for w in units],
        vm((2, 128, HD), BF),
        *[vm((2, NZ, 16, HD), BF) for _ in range(4)],
        vm((2, NY, 2, NX, 16, COLS), BF),
        vm((2, NY, 2, 9, 32, 128), F32),
        vm((2, 2, 4, 9, 32, 128), BF), vm((2, 2, 4, 9, 32, 128), BF),
        pltpu.SemaphoreType.DMA((8,)), pltpu.SemaphoreType.DMA((SEND_SLOTS,)), pltpu.SemaphoreType.DMA((RING + 32,)),
    ]
    hbm = pl.BlockSpec(memory_space=pl.ANY)
    result = pl.pallas_call(
        kernel,
        out_shape=jax.ShapeDtypeStruct((128, D_LOC), BF),
        in_specs=[hbm] * 7,
        out_specs=pl.BlockSpec(memory_space=pltpu.VMEM),
        scratch_shapes=scratch,
        compiler_params=pltpu.CompilerParams(
            collective_id=0, has_side_effects=True, vmem_limit_bytes=56 * 2**20
        ),
        cost_estimate=pl.CostEstimate(flops=4 * 10**9, bytes_accessed=10**7, transcendentals=10**6),
        name="layer",
    )(
        tokens.transpose(1, 2, 0), w_query, w_keyval.T, w_out.T, cache_keys, cache_values, lengths
    )
    return result.reshape(64, 2, D_LOC)


def solution(mesh):
    placed = (
        P(None, None, ("batch", "gy")),
        P(("batch", "gy"), "gx"),
        P(("batch", "gy"), "gx"),
        P("gx", ("batch", "gy")),
        P(("batch", "gx", "gy"), None, None),
        P(("batch", "gx", "gy"), None, None),
        P(("batch", "gx", "gy")),
    )
    return jax.shard_map(
        local, mesh=mesh, in_specs=placed, out_specs=P("gx", None, ("batch", "gy")), check_vma=False
    )
```

time: 82.9 us -> 68.5 us (0.83)
  Pallas kernels: 79.9 us -> 66.7 us
  local copies, waits for them, and re-layouts: 2.9 us -> 1.65 us
    pallas_call x1, Pallas kernels: 79.9 us -> 66.7 us  [local(): pl.pallas_call(kernel, out_shape=jax.ShapeDtypeStruct((128, D_LOC), BF),...]
    another operation x1 -> x0, local copies, waits for them, and re-layouts: 1.25 us -> none
where the time goes in v2:
time: 68.5 us; the launch traced here: 68.4 us
  Pallas kernels  66.7 us (97%)
  local copies, waits for them, and re-layouts  1.65 us (2%)
    pallas_call x1, Pallas kernels, local(): pl.pallas_call(kernel, out_shape=jax.ShapeDtypeStruct((128, D_LOC), BF),...  66.7 us
    reshape x1, local copies, waits for them, and re-layouts, local(): return result.reshape(64, 2, D_LOC)  1.65 us

profile of v2, /device:TPU:32, one launch (start us, length us, event | category | flops | bytes accessed | tf_op | source)
XLA Modules:
  0.0 68.4 jit_solution(6630487115649111008)
XLA Ops:
  0.0 66.7 %layer.1 = bf16[128,576]{1,0:T(8,128)(2,1)} custom-call(bf16[2,576,512]{2,1,0:T(8,128)(2,1)} %bitcast.4, bf16[576,1536]{1,0:T(8,128)(2,1)} %wq.1, bf16[64,576]{1,0:T(8,128)(2,1)} %bitcast.5, bf16[576,1536]{1,0:T(8,128)(2,1)} %bitcast.3, bf16[2,2048,256]{2,1,0:T(8,128)(2,1)} %ck.1, bf16[2,2048,256]{2,1,0:T(8,128)(2,1)} %cv.1, s32[2]{0:T(128)} %lens_in.1), custom_call_target="tpu_custom_call" | custom-call | flops 4000000000 | bytes 10000000 | tf_op jit(solution)/shard_map/layer/pallas_call | solution.py:395
  66.8 1.7 %reshape.3 = bf16[64,2,576]{2,1,0:T(2,128)(2,1)} reshape(bf16[128,576]{1,0:T(8,128)(2,1)} %layer.1) | data formatting | bytes 294912 | tf_op jit(solution)/shard_map/reshape | solution.py:409

commit v3 on v2

--- a/solution.py
+++ b/solution.py
@@ -14,8 +14,9 @@
 NX, NY, NZ = 4, 4, 8
 D_LOC, COLS = 576, 1536
 HD, SLOTS = 256, 2048
-SEND_SLOTS = 32
-SWAP, STAGE1, STAGE2, QUERIES, RESULTS, GATHER1, FORWARD, GATHER2, RING = 0, 4, 8, 12, 14, 16, 18, 20, 32
+SEND_SLOTS = 40
+SWAP, STAGE1, STAGE2, QUERIES, RESULTS, GATHER1, FORWARD, GATHER2, RING, RELAY = 0, 4, 8, 12, 14, 16, 28, 30, 42, 74
+RELAYED = (0, 1, 2, 3)
 LEFT, RIGHT = 768, 896
 
 
@@ -118,6 +119,7 @@
     loads["wq"].wait()
     loads["wkv"].wait()
 
+    first_two, last_two = pl.ds(0, 2), pl.ds(2, 2)
     parts, gots = (part0, part1, part2, part3), (got0, got1, got2, got3)
     mids, fins = (mid0, mid1, mid2, mid3), (fin0, fin1, fin2, fin3)
     first_x = (True, False, False, True)
@@ -154,14 +156,30 @@
                 lead = (xx, yy) if first_x[u] else (yy, xx)
                 parts[u][lead[0], lead[1]] = total[at:at + 16]
         me, to = (x, at_x) if first_x[u] else (y, at_y)
-        for o in (2, 1, 3):
-            copy_to(parts[u].at[(me + o) % 4], gots[u].at[o - 1], to(o), STAGE1 + u)
+        if u not in RELAYED:
+            for o in (2, 1, 3):
+                copy_to(parts[u].at[(me + o) % 4], gots[u].at[o - 1], to(o), STAGE1 + u)
+            return
+        ahead, far, behind = (me + 1) % 4, (me + 2) % 4, (me + 3) % 4
+        copy_to(parts[u].at[far, first_two], gots[u].at[2, first_two], to(1), RELAY + 2 * u)
+        copy_to(parts[u].at[far, last_two], gots[u].at[2, last_two], to(3), RELAY + 2 * u + 1)
+        copy_to(parts[u].at[ahead, last_two], gots[u].at[0, last_two], to(1), STAGE1 + u)
+        copy_to(parts[u].at[behind, first_two], gots[u].at[1, first_two], to(3), STAGE1 + u)
+
+    def relay_unit(u):
+        me, to = (x, at_x) if first_x[u] else (y, at_y)
+        for way, half, o in ((0, first_two, 1), (1, last_two, 3)):
+            arrived(gots[u].at[2, half], RELAY + 2 * u + way)
+            mine = parts[u].at[(me + o) % 4, half]
+            mine[...] = (mine[...].astype(F32) + gots[u][2, half].astype(F32)).astype(BF)
+            copy_to(mine, gots[u].at[way, half], to(o), STAGE1 + u)
 
     def middle_unit(u):
         me, to, other = (x, at_y, y) if first_x[u] else (y, at_x, x)
-        arrived(gots[u], STAGE1 + u)
+        came = 2 if u in RELAYED else 3
+        arrived(gots[u].at[pl.ds(0, came)], STAGE1 + u)
         total = parts[u][me].astype(F32)
-        for o in range(3):
+        for o in range(came):
             total = total + gots[u][o].astype(F32)
         mids[u][...] = total.astype(BF)
         for o in (2, 1, 3):
@@ -256,22 +274,25 @@
         mine_l = g.at[s, y, c, x, :, halves[0]]
         mine_r = g.at[s, y, c, x, :, halves[1]]
         for o in (2, 1, 3):
-            copy_to(mine_l, mine_l, at_x(o), GATHER1 + s)
-            copy_to(mine_r, mine_r, at_y(o), GATHER1 + s)
+            copy_to(mine_l, mine_l, at_x(o), GATHER1 + s * 6 + o - 1)
+            copy_to(mine_r, mine_r, at_y(o), GATHER1 + s * 6 + o + 2)
         copy_to(g.at[s, y, c, x], g.at[s, y, c, x], sibling, FORWARD + s)
+        for o in (2, 1, 3):
+            copy_to(mine_l, mine_l, at_y(o), GATHER2 + s * 6 + o - 1)
+            copy_to(mine_r, mine_r, at_x(o), GATHER2 + s * 6 + o + 2)
 
     def gather_middle(s):
-        arrived(g.at[s, 0, 0, pl.ds(0, 3)], GATHER1 + s)
-        block_l = g.at[s, y, c, :, :, halves[0]]
-        block_r = g.at[s, :, c, x, :, halves[1]]
-        for o in (2, 1, 3):
-            copy_to(block_l, block_l, at_y(o), GATHER2 + s * 6 + o - 1)
-            copy_to(block_r, block_r, at_x(o), GATHER2 + s * 6 + o + 2)
-        for o in (1, 2, 3):
-            piece = g.at[s, y, c, (x + o) % NX, :, halves[0]]
-            copy_to(piece, piece, sibling, FORWARD + s)
-            piece = g.at[s, (y + o) % NY, c, x, :, halves[1]]
-            copy_to(piece, piece, sibling, FORWARD + s)
+        for come in (1, 3, 2):
+            piece_l = g.at[s, y, c, (x + 4 - come) % NX, :, halves[0]]
+            piece_r = g.at[s, (y + 4 - come) % NY, c, x, :, halves[1]]
+            arrived(piece_l, GATHER1 + s * 6 + come - 1)
+            for o in (2, 1, 3):
+                copy_to(piece_l, piece_l, at_y(o), GATHER2 + s * 6 + o - 1)
+            copy_to(piece_l, piece_l, sibling, FORWARD + s)
+            arrived(piece_r, GATHER1 + s * 6 + come + 2)
+            for o in (2, 1, 3):
+                copy_to(piece_r, piece_r, at_x(o), GATHER2 + s * 6 + o + 2)
+            copy_to(piece_r, piece_r, sibling, FORWARD + s)
 
     def gather_end(s):
         for o in (1, 3, 2):
@@ -338,19 +359,50 @@
         ends[s] = total.astype(BF)
 
     steps = [
-        (swap_unit, 0), (swap_unit, 1), (start_unit, 0), (start_unit, 1),
-        (swap_unit, 2), (swap_unit, 3), (start_unit, 2), (start_unit, 3),
-        (middle_unit, 0), (middle_unit, 1), (middle_unit, 2), (middle_unit, 3),
-        (send_queries, 0), (send_queries, 1), (attention, 0), (attention, 1),
-        (gather_start, 0), (gather_start, 1), (gather_middle, 0), (gather_middle, 1),
-        (gather_end, 0), (output_terms, 0, 0), (output_terms, 0, 1), (ring_start, 0),
-        (gather_end, 1), (output_terms, 1, 0), (output_terms, 1, 1), (ring_start, 1),
-        (ring_step, 0, 1, True), (ring_step, 0, 2, False),
-        (ring_step, 1, 1, True), (ring_step, 1, 2, False),
-        (ring_step, 0, 2, True), (ring_step, 0, 3, False),
-        (ring_step, 1, 2, True), (ring_step, 1, 3, False),
-        (ring_step, 0, 3, True), (ring_step, 1, 3, True),
-        (ring_end, 0), (ring_end, 1),
+        (swap_unit, 0),
+        (swap_unit, 1),
+        (start_unit, 0),
+        (start_unit, 1),
+        (swap_unit, 3),
+        (swap_unit, 2),
+        (start_unit, 3),
+        (start_unit, 2),
+        (relay_unit, 0),
+        (relay_unit, 1),
+        (relay_unit, 3),
+        (relay_unit, 2),
+        (middle_unit, 0),
+        (middle_unit, 1),
+        (middle_unit, 3),
+        (middle_unit, 2),
+        (send_queries, 0),
+        (send_queries, 1),
+        (attention, 0),
+        (attention, 1),
+        (gather_start, 0),
+        (gather_start, 1),
+        (gather_middle, 0),
+        (gather_middle, 1),
+        (gather_end, 0),
+        (output_terms, 0, 0),
+        (output_terms, 0, 1),
+        (ring_start, 0),
+        (gather_end, 1),
+        (output_terms, 1, 0),
+        (output_terms, 1, 1),
+        (ring_start, 1),
+        (ring_step, 0, 1, True),
+        (ring_step, 0, 2, False),
+        (ring_step, 1, 1, True),
+        (ring_step, 1, 2, False),
+        (ring_step, 0, 2, True),
+        (ring_step, 0, 3, False),
+        (ring_step, 1, 2, True),
+        (ring_step, 1, 3, False),
+        (ring_step, 0, 3, True),
+        (ring_step, 1, 3, True),
+        (ring_end, 0),
+        (ring_end, 1),
     ]
     for function, *arguments in steps:
         function(*arguments)
@@ -389,7 +441,7 @@
         vm((2, NY, 2, NX, 16, COLS), BF),
         vm((2, NY, 2, 9, 32, 128), F32),
         vm((2, 2, 4, 9, 32, 128), BF), vm((2, 2, 4, 9, 32, 128), BF),
-        pltpu.SemaphoreType.DMA((8,)), pltpu.SemaphoreType.DMA((SEND_SLOTS,)), pltpu.SemaphoreType.DMA((RING + 32,)),
+        pltpu.SemaphoreType.DMA((8,)), pltpu.SemaphoreType.DMA((SEND_SLOTS,)), pltpu.SemaphoreType.DMA((RELAY + 8,)),
     ]
     hbm = pl.BlockSpec(memory_space=pl.ANY)
     result = pl.pallas_call(

time: 68.5 us -> 67.6 us (0.987)
  Pallas kernels: 66.7 us -> 65.8 us
    pallas_call x1, Pallas kernels: 66.7 us -> 65.8 us  [local(): pl.pallas_call(kernel, out_shape=jax.ShapeDtypeStruct((128, D_LOC), BF),...]
where the time goes in v3:
time: 67.6 us; the launch traced here: 67.5 us
  Pallas kernels  65.8 us (97%)
  local copies, waits for them, and re-layouts  1.65 us (2%)
    pallas_call x1, Pallas kernels, local(): pl.pallas_call(kernel, out_shape=jax.ShapeDtypeStruct((128, D_LOC), BF),...  65.8 us
    reshape x1, local copies, waits for them, and re-layouts, local(): return result.reshape(64, 2, D_LOC)  1.65 us

profile of v3, /device:TPU:32, one launch (start us, length us, event | category | flops | bytes accessed | tf_op | source)
XLA Modules:
  0.0 67.5 jit_solution(8966406069662185977)
XLA Ops:
  0.0 65.8 %layer.1 = bf16[128,576]{1,0:T(8,128)(2,1)} custom-call(bf16[2,576,512]{2,1,0:T(8,128)(2,1)} %bitcast.4, bf16[576,1536]{1,0:T(8,128)(2,1)} %wq.1, bf16[64,576]{1,0:T(8,128)(2,1)} %bitcast.5, bf16[576,1536]{1,0:T(8,128)(2,1)} %bitcast.3, bf16[2,2048,256]{2,1,0:T(8,128)(2,1)} %ck.1, bf16[2,2048,256]{2,1,0:T(8,128)(2,1)} %cv.1, s32[2]{0:T(128)} %lens_in.1), custom_call_target="tpu_custom_call" | custom-call | flops 4000000000 | bytes 10000000 | tf_op jit(solution)/shard_map/layer/pallas_call | solution.py:447
  65.8 1.7 %reshape.3 = bf16[64,2,576]{2,1,0:T(2,128)(2,1)} reshape(bf16[128,576]{1,0:T(8,128)(2,1)} %layer.1) | data formatting | bytes 294912 | tf_op jit(solution)/shard_map/reshape | solution.py:461

commit v4 on v3

--- a/solution.py
+++ b/solution.py
@@ -14,7 +14,7 @@
 NX, NY, NZ = 4, 4, 8
 D_LOC, COLS = 576, 1536
 HD, SLOTS = 256, 2048
-SEND_SLOTS = 40
+SEND_SLOTS = 28
 SWAP, STAGE1, STAGE2, QUERIES, RESULTS, GATHER1, FORWARD, GATHER2, RING, RELAY = 0, 4, 8, 12, 14, 16, 28, 30, 42, 74
 RELAYED = (0, 1, 2, 3)
 LEFT, RIGHT = 768, 896
@@ -282,7 +282,7 @@
             copy_to(mine_r, mine_r, at_x(o), GATHER2 + s * 6 + o + 2)
 
     def gather_middle(s):
-        for come in (1, 3, 2):
+        for come in (1, 2, 3):
             piece_l = g.at[s, y, c, (x + 4 - come) % NX, :, halves[0]]
             piece_r = g.at[s, (y + 4 - come) % NY, c, x, :, halves[1]]
             arrived(piece_l, GATHER1 + s * 6 + come - 1)
@@ -385,19 +385,19 @@
         (gather_middle, 1),
         (gather_end, 0),
         (output_terms, 0, 0),
+        (gather_end, 1),
         (output_terms, 0, 1),
         (ring_start, 0),
-        (gather_end, 1),
         (output_terms, 1, 0),
         (output_terms, 1, 1),
         (ring_start, 1),
         (ring_step, 0, 1, True),
+        (ring_step, 1, 1, True),
         (ring_step, 0, 2, False),
-        (ring_step, 1, 1, True),
         (ring_step, 1, 2, False),
         (ring_step, 0, 2, True),
+        (ring_step, 1, 2, True),
         (ring_step, 0, 3, False),
-        (ring_step, 1, 2, True),
         (ring_step, 1, 3, False),
         (ring_step, 0, 3, True),
         (ring_step, 1, 3, True),

time: 67.6 us -> 67.2 us (level)
  no operation moved by 1% of the time
where the time goes in v4:
time: 67.2 us; the launch traced here: 66.8 us
  Pallas kernels  65.2 us (97%)
  local copies, waits for them, and re-layouts  1.65 us (2%)
    pallas_call x1, Pallas kernels, local(): pl.pallas_call(kernel, out_shape=jax.ShapeDtypeStruct((128, D_LOC), BF),...  65.2 us
    reshape x1, local copies, waits for them, and re-layouts, local(): return result.reshape(64, 2, D_LOC)  1.65 us

profile of v4, /device:TPU:32, one launch (start us, length us, event | category | flops | bytes accessed | tf_op | source)
XLA Modules:
  0.0 66.8 jit_solution(952198776536264636)
XLA Ops:
  0.0 65.2 %layer.1 = bf16[128,576]{1,0:T(8,128)(2,1)} custom-call(bf16[2,576,512]{2,1,0:T(8,128)(2,1)} %bitcast.4, bf16[576,1536]{1,0:T(8,128)(2,1)} %wq.1, bf16[64,576]{1,0:T(8,128)(2,1)} %bitcast.5, bf16[576,1536]{1,0:T(8,128)(2,1)} %bitcast.3, bf16[2,2048,256]{2,1,0:T(8,128)(2,1)} %ck.1, bf16[2,2048,256]{2,1,0:T(8,128)(2,1)} %cv.1, s32[2]{0:T(128)} %lens_in.1), custom_call_target="tpu_custom_call" | custom-call | flops 4000000000 | bytes 10000000 | tf_op jit(solution)/shard_map/layer/pallas_call | solution.py:447
  65.2 1.7 %reshape.3 = bf16[64,2,576]{2,1,0:T(2,128)(2,1)} reshape(bf16[128,576]{1,0:T(8,128)(2,1)} %layer.1) | data formatting | bytes 294912 | tf_op jit(solution)/shard_map/reshape | solution.py:461

commit v5 on v4

--- a/solution.py
+++ b/solution.py
@@ -45,7 +45,7 @@
     sib_s, sib_r, part0, part1, part2, part3, got0, got1, got2, got3,
     mid0, mid1, mid2, mid3, fin0, fin1, fin2, fin3,
     stack, qs, qr, ats, atr, g, zpart, zs, zr,
-    ld_sem, send_sem, recv_sem,
+    vwt, ld_sem, send_sem, recv_sem,
 ):
     b = lax.axis_index("batch")
     z = lax.axis_index("gx")
@@ -239,16 +239,15 @@
                 [u * cos_rows - w * sin_rows, w * cos_rows + u * sin_rows], axis=1
             ).astype(BF)
 
-        queries = rotate(raw.astype(F32))
+        queries = rotate(raw.astype(F32)) * (1.0 / HD**0.5)
         new_keys = rotate(dot_nn(pick_key, raw))
         new_values = dot_nn(pick_value, raw).astype(BF)
         if s == 0:
             loads["k"].wait()
-        scale = 1.0 / HD**0.5
-        cached = dot_nt(queries, vk[s]) * scale
+        cached = dot_nt(queries, vk[s])
         _, column = grid_of(128, SLOTS)
         cached = jnp.where(column < lens[s], cached, -1e30)
-        fresh = jnp.where(causal, dot_nt(queries, new_keys) * scale, -1e30)
+        fresh = jnp.where(causal, dot_nt(queries, new_keys), -1e30)
         highest = jnp.maximum(cached.max(-1, keepdims=True), fresh.max(-1, keepdims=True))
         cached = jnp.exp(cached - highest)
         fresh = jnp.exp(fresh - highest)
@@ -305,15 +304,17 @@
 
     low = lax.broadcasted_iota(jnp.int32, (32, 128), 1) < 64
 
+    def prepare_output():
+        loads["wo"].wait()
+        loads["wo2"].wait()
+        for n in range(6):
+            vwt[n * 256:(n + 1) * 256] = vwo[:, n * 256:(n + 1) * 256].T
+
     def output_terms(s, core):
-        if core == 0:
-            if s == 0:
-                loads["wo"].wait()
-                loads["wo2"].wait()
-        else:
+        if core == 1:
             arrived(g.at[s, :, 1 - c], FORWARD + s)
         core = c if core == 0 else 1 - c
-        terms = dot_nt(g[s, :, core].reshape(256, COLS), vwo[...])
+        terms = dot_nn(g[s, :, core].reshape(256, COLS), vwt[...])
         for yy in range(NY):
             mine = terms[yy * 64:(yy + 1) * 64]
             for cb in range(4):
@@ -367,6 +368,7 @@
         (swap_unit, 2),
         (start_unit, 3),
         (start_unit, 2),
+        (prepare_output,),
         (relay_unit, 0),
         (relay_unit, 1),
         (relay_unit, 3),
@@ -441,6 +443,7 @@
         vm((2, NY, 2, NX, 16, COLS), BF),
         vm((2, NY, 2, 9, 32, 128), F32),
         vm((2, 2, 4, 9, 32, 128), BF), vm((2, 2, 4, 9, 32, 128), BF),
+        vm((COLS, 640), BF),
         pltpu.SemaphoreType.DMA((8,)), pltpu.SemaphoreType.DMA((SEND_SLOTS,)), pltpu.SemaphoreType.DMA((RELAY + 8,)),
     ]
     hbm = pl.BlockSpec(memory_space=pl.ANY)

time: 67.2 us -> 66.6 us (level)
  Pallas kernels: 65.2 us -> 64.5 us
where the time goes in v5:
time: 66.6 us; the launch traced here: 66.2 us
  Pallas kernels  64.5 us (97%)
  local copies, waits for them, and re-layouts  1.65 us (2%)
    pallas_call x1, Pallas kernels, local(): pl.pallas_call(kernel, out_shape=jax.ShapeDtypeStruct((128, D_LOC), BF),...  64.5 us
    reshape x1, local copies, waits for them, and re-layouts, local(): return result.reshape(64, 2, D_LOC)  1.65 us

profile of v5, /device:TPU:32, one launch (start us, length us, event | category | flops | bytes accessed | tf_op | source)
XLA Modules:
  0.0 66.2 jit_solution(911853695080660020)
XLA Ops:
  0.0 64.5 %layer.1 = bf16[128,576]{1,0:T(8,128)(2,1)} custom-call(bf16[2,576,512]{2,1,0:T(8,128)(2,1)} %bitcast.4, bf16[576,1536]{1,0:T(8,128)(2,1)} %wq.1, bf16[64,576]{1,0:T(8,128)(2,1)} %bitcast.5, bf16[576,1536]{1,0:T(8,128)(2,1)} %bitcast.3, bf16[2,2048,256]{2,1,0:T(8,128)(2,1)} %ck.1, bf16[2,2048,256]{2,1,0:T(8,128)(2,1)} %cv.1, s32[2]{0:T(128)} %lens_in.1), custom_call_target="tpu_custom_call" | custom-call | flops 4000000000 | bytes 10000000 | tf_op jit(solution)/shard_map/layer/pallas_call | solution.py:450
  64.6 1.7 %reshape.3 = bf16[64,2,576]{2,1,0:T(2,128)(2,1)} reshape(bf16[128,576]{1,0:T(8,128)(2,1)} %layer.1) | data formatting | bytes 294912 | tf_op jit(solution)/shard_map/reshape | solution.py:464
